TPU v7x, 256 devices: a whole 4x4x8 slice. The times are simulated.
256 devices in a mesh: replica: 8 (over x_hi, y), fsdp: 32 (over x_lo, z, core).
Axes of the slice: x: 4 (x_hi: 2, x_lo: 2; x = x_hi * 2 + x_lo), y: 4, z: 8, core: 2. Of those that a mesh axis runs over, the one named last changes fastest.
Arguments:
- activations: bfloat16 [98304, 4096], P(('replica', 'fsdp')), may hold values from -24 to 24
- cotangent: bfloat16 [98304, 1024], P(('replica', 'fsdp')), may hold values from -6 to 6
- inner_weight: bfloat16 [8, 4096, 1024], P('replica', 'fsdp'), may hold values from -0.09375 to 0.09375
- outer_params: float32 [4096, 1024], P('fsdp'), may hold values from -6 to 6
- replica_params: float32 [8, 4096, 1024], P('replica', 'fsdp'), may hold values from -6 to 6
- momentum: float32 [4096, 1024], P('fsdp'), may hold values from -3 to 3
Outputs:
- values: bfloat16 [98304, 1024], P(('replica', 'fsdp'))
- input_grad: bfloat16 [98304, 4096], P(('replica', 'fsdp'))
- weight_grad: float32 [8, 4096, 1024], P('replica', 'fsdp')
- new_params: float32 [4096, 1024], P('fsdp')
- new_momentum: float32 [4096, 1024], P('fsdp')
All inputs are finite; a program needn't handle non-finite values.
Results may differ from a plain program's by a relative error of at most 0.001.
Values may be sent and summed in bfloat16 or wider, within the bound.
A program may use at most 128 MiB of HBM per device.

v0:
```python
import math

import jax
import jax.numpy as jnp
from jax import lax
from jax.sharding import PartitionSpec as P


def local(activations, cotangent, inner_weight, outer_params, replica_params, momentum):
    weight_shard = inner_weight[0]
    token_count = activations.shape[0]
    feature_cols = activations
    outputs = jnp.dot(
        feature_cols,
        lax.all_gather(weight_shard, "fsdp", axis=0, tiled=True),
        preferred_element_type=jnp.float32,
    )
    input_back = lax.dot_general(
        cotangent,
        lax.all_gather(weight_shard, "fsdp", axis=0, tiled=True),
        (((1,), (1,)), ((), ())),
        preferred_element_type=jnp.float32,
    )
    grad_scale = 1.0 / math.sqrt(token_count * lax.axis_size("fsdp"))
    feature_cols = activations
    weight_grad = (
        lax.psum_scatter(
            lax.dot_general(
                feature_cols,
                cotangent,
                (((0,), (0,)), ((), ())),
                preferred_element_type=jnp.float32,
            ),
            "fsdp",
            scatter_dimension=0,
            tiled=True,
        )
        * grad_scale
    )
    difference = outer_params - replica_params[0]
    replicas = lax.axis_size("replica")
    outer_grad = lax.psum(difference, "replica") / replicas
    new_momentum = 0.9 * momentum + outer_grad
    new_params = outer_params - 0.7 * (outer_grad + 0.9 * new_momentum)
    return (
        outputs.astype(jnp.bfloat16),
        input_back.astype(jnp.bfloat16),
        weight_grad[None],
        new_params,
        new_momentum,
    )


def solution(mesh):
    placed = (
        P(("replica", "fsdp"), None),
        P(("replica", "fsdp"), None),
        P("replica", "fsdp", None),
        P("fsdp", None),
        P("replica", "fsdp", None),
        P("fsdp", None),
    )
    return jax.shard_map(
        local,
        mesh=mesh,
        in_specs=placed,
        out_specs=(
            P(("replica", "fsdp"), None),
            P(("replica", "fsdp"), None),
            P("replica", "fsdp", None),
            P("fsdp", None),
            P("fsdp", None),
        ),
        check_vma=False,
    )
```

profile of v0, /device:TPU:16, one launch (start us, length us, event | category | flops | bytes accessed | tf_op | source)
XLA Modules:
  0.0 244.1 jit_solution(17061468780316685483)
XLA Ops:
  8.0 0.0 copy-start
  8.0 0.0 all-reduce.2.cloned.1.call-start
  8.1 2.2 bitcast_subtract_fusion
  10.3 0.0 all-reduce.2.cloned.1.call-update
  10.3 0.0 all-gather.3.cloned.1.call-start
  10.3 0.5 all-gather.3.cloned.1.call-update
  10.9 0.0 reduce-scatter.2.cloned.1.call-start
  10.9 0.0 copy-done
  10.9 9.3 %fusion.10 = f32[4096,1024]{1,0:T(8,128)} fusion(bf16[384,4096]{1,0:T(8,128)(2,1)S(1)} %copy-done, bf16[384,1024]{1,0:T(8,128)(2,1)} %param.7), kind=kOutput, calls=%fused_computation.10 | convolution fusion | flops 3221225472 | bytes 20709376 | tf_op jit(solution)/shard_map/dot_general | solution.py:28
  20.2 0.0 reduce-scatter.2.cloned.1.call-update
  20.2 83.6 %all-reduce.2.cloned.1.call-done = f32[128,1024]{1,0:T(8,128)} async-done(((f32[128,1024]{1,0:T(8,128)}), f32[128,1024]{1,0:T(8,128)}) %all-reduce.2.cloned.1.call-update) | async-done | bytes 524304 | tf_op jit(solution)/shard_map/psum | solution.py:42
  103.9 2.5 %multiply_subtract_fusion = (f32[128,1024]{1,0:T(8,128)}, f32[128,1024]{1,0:T(8,128)}) fusion(f32[128,1024]{1,0:T(8,128)} %param.9, f32[128,1024]{1,0:T(8,128)} %all-reduce.2.cloned.1.call-done, f32[128,1024]{1,0:T(8,128)} %param.11), kind=kLoop, calls=%fused_computation.7 | loop fusion | flops 917504 | bytes 2621440 | tf_op jit(solution)/shard_map/sub | solution.py:44
  106.4 0.0 all-gather.3.cloned.1.call-done
  106.4 0.0 copy-start.1
  106.4 9.0 %fusion.4 = bf16[384,4096]{1,0:T(8,128)(2,1)} fusion(bf16[384,1024]{1,0:T(8,128)(2,1)} %param.7, bf16[1,4096,1024]{2,1,0:T(8,128)(2,1)} %all-gather.3.cloned.1.call-done), kind=kOutput, calls=%fused_computation.4 | convolution fusion | flops 3222798336 | bytes 12320768 | tf_op jit(solution)/shard_map/dot_general | solution.py:18
  115.4 0.0 copy-done.1
  115.4 4.4 %fusion.7 = bf16[384,1024]{1,0:T(8,128)(2,1)} fusion(bf16[384,4096]{1,0:T(8,128)(2,1)S(1)} %copy-done, bf16[1,4096,1024]{2,1,0:T(8,128)(2,1)S(1)} %copy-done.1), kind=kOutput, calls=%fused_computation.5 | convolution fusion | flops 3221618688 | bytes 12320768 | tf_op jit(solution)/shard_map/dot_general | solution.py:13
  119.8 115.0 %reduce-scatter.2.cloned.1.call-done = f32[128,1024]{1,0:T(8,128)} async-done(((f32[4096,1024]{1,0:T(8,128)}), f32[128,1024]{1,0:T(8,128)}) %reduce-scatter.2.cloned.1.call-update) | async-done | bytes 524304 | tf_op jit(solution)/shard_map/reduce_scatter | solution.py:27
  234.8 1.9 multiply_bitcast_fusion
Async XLA Ops:
  8.0 2.9 %copy-start = (bf16[384,4096]{1,0:T(8,128)(2,1)S(1)}, bf16[384,4096]{1,0:T(8,128)(2,1)}, u32[]{:S(2)}) copy-start(bf16[384,4096]{1,0:T(8,128)(2,1)} %param.6) | copy-start | bytes 9437188
  8.0 95.9 %all-reduce.2.cloned.1.call-start = ((), (), s32[]{:S(2)}) async-start(), calls=%async_computation.2 | async-start | bytes 1048576 | tf_op jit(solution)/shard_map/psum | solution.py:42
  10.3 96.1 %all-gather.3.cloned.1.call-start = ((), (), s32[]{:S(2)}) async-start(), calls=%async_computation.3 | async-start | bytes 8650752 | tf_op jit(solution)/shard_map/all_gather | solution.py:15
  10.9 223.9 %reduce-scatter.2.cloned.1.call-start = ((), (), s32[]{:S(2)}) async-start(), calls=%async_computation.1 | async-start | bytes 17301504 | tf_op jit(solution)/shard_map/reduce_scatter | solution.py:27
  106.4 9.0 %copy-start.1 = (bf16[1,4096,1024]{2,1,0:T(8,128)(2,1)S(1)}, bf16[1,4096,1024]{2,1,0:T(8,128)(2,1)}, u32[]{:S(2)}) copy-start(bf16[1,4096,1024]{2,1,0:T(8,128)(2,1)} %all-gather.3.cloned.1.call-done) | copy-start | bytes 25165828
Sparse Core Ops, SparseCore 0:
  12.1 91.7 all-reduce.1
Sparse Core Ops, SparseCore 1:
  12.6 75.7 all-gather.2
  90.8 143.9 reduce-scatter.1
where the time goes:
time: 244 us
  waiting for transfers between devices  199 us (82%)
  matrix products  22.7 us (9%)
  between operations  15.5 us (6%)
  other arithmetic  6.64 us (3%)
    reduce_scatter x1, waiting for transfers between devices, local(): lax.psum_scatter(lax.dot_general(feature_cols, cotangent, (((0,), (0,)),...  115 us
    psum x1, waiting for transfers between devices, local(): outer_grad = lax.psum(difference, 'replica') / replicas  83.6 us
    dot_general x1, matrix products, local(): lax.dot_general(feature_cols, cotangent, (((0,), (0,)), ((), ())), prefer...  9.27 us
    dot_general x1, matrix products, local(): lax.dot_general(cotangent, lax.all_gather(weight_shard, 'fsdp', axis=0, t...  9.02 us
  transfers between devices with their start and end apart: 3, of which 2 were waited for; matrix products, arithmetic and copies ran while one was open for 10% of the time, Pallas kernels for 0%

commit v1 on v0

v1 whole, which is shorter than its diff:
```python
import functools
import math

import jax
import jax.numpy as jnp
from jax import lax
from jax.experimental import pallas as pl
from jax.experimental.pallas import tpu as pltpu
from jax.sharding import PartitionSpec as P

MESH = pl.DeviceIdType.MESH
F32 = jnp.float32
BF16 = jnp.bfloat16

NZ = 8
SH = 128
HF = 64
QT = 32
BLK = 16


def encode(v):
    a = v * v
    b = a * a
    return (b * a * (v * jnp.abs(v))).astype(BF16)


def decode(q):
    t = q.astype(F32)
    a = lax.rsqrt(lax.rsqrt(jnp.maximum(jnp.abs(t), 1e-37)))
    r = a * lax.rsqrt(a)
    return jnp.where(t < 0, -r, r)


def kernel(
    grad_scale,
    x_in, g_in, w_in, op_in, rp_in, mom_in,
    val_out, dx_out, dw_out, np_out, nm_out,
    xv, xs, gs, W, part, zq, zr, xq, xr, dxv, acc, valv, dwv,
    opv, rpv, momv, diff, ryv, xhv, tot, mine, mxr, mzr,
    load_sem, xs_sem, out_sem, dx_sem,
    agz_s, agz_r, agx_s, agx_r, sib_s, sib_r, tok_s, tok_r,
    rsz_s, rsz_r, rsx_s, rsx_r, mx_s, mx_r, rep_s, rep_r,
):
    r = lax.axis_index("replica")
    f = lax.axis_index("fsdp")
    xh, y = r // 4, r % 4
    x, z, c = f // 16, (f // 2) % NZ, f % 2
    ox, oc = 1 - x, 1 - c

    def zmod(v):
        return (v + 2 * NZ) % NZ

    def dev(xx, zz, cc):
        return (r, xx * 16 + zz * 2 + cc)

    def rep(hh, yy):
        return (hh * 4 + yy, f)

    def idx(xx, zz):
        return xx * NZ + zz

    x_nb, sib = dev(ox, z, c), dev(x, z, oc)
    z_nb = (dev(x, zmod(z + 1), c), dev(x, zmod(z - 1), c))
    xh_nb = rep(1 - xh, y)

    def remote(src, dst, ss, rs, to):
        return pltpu.make_async_remote_copy(
            src_ref=src, dst_ref=dst, send_sem=ss, recv_sem=rs, device_id=to, device_id_type=MESH
        )

    def cols(j, cc):
        return pl.ds(pl.multiple_of(j * 256 + cc * SH, SH), SH)

    loads = [
        pltpu.make_async_copy(w_in.at[0], W.at[idx(x, z), pl.ds(pl.multiple_of(c * SH, SH), SH)], load_sem.at[0]),
        pltpu.make_async_copy(op_in, opv, load_sem.at[1]),
        pltpu.make_async_copy(rp_in.at[0], rpv, load_sem.at[2]),
        pltpu.make_async_copy(g_in, gs.at[pl.ds(0, 384)], load_sem.at[3]),
        pltpu.make_async_copy(x_in, xv, load_sem.at[4]),
        pltpu.make_async_copy(mom_in, momv, load_sem.at[5]),
    ]
    for copy in loads[:4]:
        copy.start()

    barrier = pltpu.get_barrier_semaphore()
    peers = [x_nb, sib, xh_nb]
    peers += [dev(x, zmod(z + j), c) for j in range(1, NZ)]
    peers += [rep(xh, (y + j) % 4) for j in range(1, 4)]
    for peer in peers:
        pl.semaphore_signal(barrier, inc=1, device_id=peer, device_id_type=MESH)
    pl.semaphore_wait(barrier, len(peers))

    def rows(p, k=1, way=0):
        if p == 1:
            if k == 4:
                return HF + QT * way, QT
            return HF, HF
        return 0, HF

    def wpiece(xx, zz, start, size, cc=None):
        cc = c if cc is None else cc
        return W.at[idx(xx, zz), pl.ds(pl.multiple_of(cc * SH + start, QT), size)]

    def far(way, k):
        return zmod(z - k) if way == 0 else zmod(z + k)

    def ag_z(way, k, p, at):
        start, size = rows(p, k, way)
        ref = wpiece(ox if p == 2 else x, at, start, size)
        return remote(ref, ref, agz_s.at[way, k - 1, p], agz_r.at[way, k - 1, p], z_nb[way])

    def ag_z_send(way, k, p):
        ag_z(way, k, p, far(way, k - 1)).start()

    def ag_z_wait(way, k, p):
        ag_z(way, k, p, far(way, k)).wait_recv()

    def ag_x(n, xx, zz, start, size):
        ref = wpiece(xx, zz, start, size)
        return remote(ref, ref, agx_s.at[n], agx_r.at[n], x_nb)

    def b_of(way, k):
        if k == 4:
            return 8 + way, HF + QT * way, QT
        return 2 + way * 3 + k - 1, HF, HF

    def ag_b_send(way, k):
        n, start, size = b_of(way, k)
        ag_x(n, x, far(way, k), start, size).start()

    def ag_b_wait(way, k):
        n, start, size = b_of(way, k)
        ag_x(n, ox, far(way, k), start, size).wait_recv()

    def sib_copy(xrel, o, cc):
        ref = wpiece(x if xrel == 0 else ox, zmod(z + o), 0, SH, cc)
        n = xrel * NZ + o
        return remote(ref, ref, sib_s.at[n], sib_r.at[n], sib)

    loads[0].wait()
    own_a = wpiece(x, z, 0, HF)
    ag_x(0, x, z, 0, HF).start()
    for way in (0, 1):
        ag_z_send(way, 1, 0)
    ag_x(1, x, z, HF, HF).start()
    for way in (0, 1):
        ag_z_send(way, 1, 1)

    @pl.loop(0, 16)
    def _(j):
        at = pl.ds(pl.multiple_of(j * SH, SH), SH)
        remote(x_in.at[:, cols(j, oc)], xs.at[pl.ds(384, 384), at], tok_s.at[0], tok_r.at[0], sib).start()
        pltpu.make_async_copy(x_in.at[:, cols(j, c)], xs.at[pl.ds(0, 384), at], xs_sem.at[0]).start()

    tok_g = remote(g_in, gs.at[pl.ds(384, 384)], tok_s.at[1], tok_r.at[1], sib)
    tok_g.start()
    sib_copy(0, 0, c).start()
    loads[4].start()
    loads[5].start()

    loads[1].wait()
    loads[2].wait()

    @pl.loop(0, SH // BLK)
    def _(i):
        at = pl.ds(pl.multiple_of(i * BLK, BLK), BLK)
        diff[at, :] = opv[at, :] - rpv[at, :]

    def quarter(yy):
        return pl.ds(pl.multiple_of(yy * QT, QT), QT)

    def rep_scatter(j):
        to = (y + j) % 4
        return remote(diff.at[quarter(to)], ryv.at[j - 1], rep_s.at[j - 1], rep_r.at[j - 1], rep(xh, to))

    for j in range(1, 4):
        rep_scatter(j).start()

    ag_x(0, ox, z, 0, HF).wait_recv()
    for way in (0, 1):
        ag_z_send(way, 1, 2)

    loads[3].wait()
    tok_x = remote(xs.at[pl.ds(384, 384)], xs.at[pl.ds(384, 384)], tok_s.at[0], tok_r.at[0], sib)
    pltpu.make_async_copy(xs.at[pl.ds(0, 384)], xs.at[pl.ds(0, 384)], xs_sem.at[0]).wait()
    tok_g.wait_recv()
    tok_x.wait_recv()

    def partial(first, last):
        @pl.loop(first, last)
        def _(i):
            at = pl.ds(pl.multiple_of(i * 512, 512), 512)
            part[pl.ds(i * 4, 4)] = lax.dot_general(
                xs[:, at], gs[...], (((0,), (0,)), ((), ())), preferred_element_type=F32
            ).reshape(4, SH, 1024)

    def use(*offsets):
        for o in offsets:
            for xrel in (0, 1):
                sib_copy(xrel, o, oc).wait_recv()
        n = len(offsets)
        first, step = offsets[0], (offsets[1] - offsets[0] if n > 1 else 0)

        @pl.loop(0, 2 * n)
        def _(t):
            o = first + (t // 2) * step
            i = t % 2
            xx = x * (1 - i) + ox * i
            products_at(idx(xx, zmod(z + o)))

    def products_at(i):
        at = pl.ds(pl.multiple_of(i * 256, 256), 256)
        w = W[i]
        dxv[:, at] = lax.dot_general(
            gs[pl.ds(0, 384), :], w, (((1,), (1,)), ((), ())), preferred_element_type=F32
        ).astype(BF16)
        pltpu.make_async_copy(dxv.at[:, at], dx_out.at[:, at], dx_sem.at[0]).start()
        acc[...] += jnp.dot(xv[:, at], w, preferred_element_type=F32)

    def forward(k, p):
        for way in (0, 1):
            ag_z_wait(way, k, p)
            if k < 3 or p == 1 or (way, p) in ((0, 0), (1, 2)):
                ag_z_send(way, k + 1, p)
            if p == 1:
                ag_b_send(way, k)

    def off(way, k):
        return (NZ - k) % NZ if way == 0 else k

    def to_sib(k):
        for way in (0, 1):
            sib_copy(0, off(way, k), c).start()

    def to_sib_other(k):
        for way in (0, 1):
            ag_b_wait(way, k)
            sib_copy(1, off(way, k), c).start()

    partial(0, 2)
    forward(1, 0)
    partial(2, 3)
    forward(1, 1)
    to_sib(1)
    partial(3, 4)
    forward(1, 2)

    ag_x(1, ox, z, HF, HF).wait_recv()
    sib_copy(1, 0, c).start()

    mine[...] = jnp.zeros_like(mine)

    @pl.loop(0, 16 * SH // BLK)
    def _(i):
        v = jnp.abs(part[i // (SH // BLK), pl.ds(pl.multiple_of((i % (SH // BLK)) * BLK, BLK), BLK), :])
        v = jnp.maximum(v[0:8], v[8:16])
        m = mine[...]
        for j in range(8):
            m = jnp.maximum(m, v[:, j * 128 : (j + 1) * 128])
        mine[...] = m

    max_x = remote(mine, mxr, mx_s.at[0], mx_r.at[0], x_nb)
    max_x.start()

    for j in range(1, 4):
        rep_scatter(j).wait_recv()
    tot[quarter(y), :] = ((diff[quarter(y), :] + ryv[0]) + ryv[1]) + ryv[2]
    xhv[0] = tot[quarter(y), :]
    rep_x = remote(xhv.at[0], xhv.at[1], rep_s.at[3], rep_r.at[3], xh_nb)
    rep_x.start()

    max_x.wait()
    mine[...] = jnp.maximum(mine[...], mxr[...])

    def max_z(j):
        return remote(mine, mzr.at[j - 1], mx_s.at[j], mx_r.at[j], dev(x, zmod(z + j), c))

    for j in range(1, NZ):
        max_z(j).start()

    acc[...] = jnp.zeros_like(acc)
    loads[4].wait()
    forward(2, 0)
    to_sib_other(1)
    use(0)
    forward(2, 1)
    to_sib(2)
    use(1, 7)
    forward(2, 2)

    for j in range(1, NZ):
        max_z(j).wait()
    m = mine[...]
    for j in range(NZ - 1):
        m = jnp.maximum(m, mzr[j])
    top = jnp.maximum(jnp.full((8, 128), jnp.max(m), F32), 1e-30)
    scale = jnp.max(2048.0 / top)
    back = jnp.max(top * (grad_scale / 2048.0))

    def total(xx, zz, start, at, received):
        v = part[idx(xx, zz), pl.ds(pl.multiple_of(start + at, BLK), BLK), :] * scale
        for ref in received:
            v = v + decode(ref[pl.ds(pl.multiple_of(at, BLK), BLK), :])
        return v

    def summed(dst, xx, zz, start, size, received):
        @pl.loop(0, size // BLK)
        def _(i):
            at = pl.multiple_of(i * BLK, BLK)
            dst[pl.ds(at, BLK), :] = encode(total(xx, zz, start, at, received))

    def rs_x(n):
        return remote(xq.at[n], xr.at[n], rsx_s.at[n], rsx_r.at[n], x_nb)

    def rs_b_send(o):
        summed(xq.at[o], ox, zmod(z + o), HF, HF, [])
        rs_x(o).start()

    def rs_z(way, j, p):
        size = QT if (j == 0 and p == 1) else HF
        at = QT * way if (j == 0 and p == 1) else 0
        here, there = zq.at[way, j, p, pl.ds(at, size)], zr.at[way, j, p, pl.ds(at, size)]
        return remote(here, there, rsz_s.at[way, j, p], rsz_r.at[way, j, p], z_nb[way])

    def rs_send(way, j, p):
        o = 4 - j if way == 0 else (4 + j) % NZ
        zz, col = zmod(z + o), (ox if p == 2 else x)
        out, crossed = zq.at[way, j, p], xr.at[o]
        if p != 1:
            if j > 0 and not (j == 1 and (way, p) in ((0, 2), (1, 0))):
                rs_z(way, j - 1, p).wait_recv()
                received = [zr.at[way, j - 1, p]]
            else:
                received = []
            summed(out, col, zz, 0, HF, received)
        elif j >= 2:
            rs_z(way, j - 1, p).wait_recv()
            summed(out, col, zz, HF, HF, [crossed, zr.at[way, j - 1, p]])
        else:
            for half in (0, 1):
                at = pl.ds(QT * half, QT)
                if j == 0 and half == way:
                    summed(out.at[at], col, zz, HF + QT * half, QT, [crossed.at[at]])
                elif j == 1 and half == way:
                    rs_z(way, 0, p).wait_recv()
                    summed(out.at[at], col, zz, HF + QT * half, QT, [crossed.at[at], zr.at[way, 0, p, at]])
                elif j == 1:
                    summed(out.at[at], col, zz, HF + QT * half, QT, [crossed.at[at]])
        rs_z(way, j, p).start()

    for o in (4, 3, 5):
        rs_b_send(o)

    forward(3, 0)
    forward(3, 1)
    to_sib_other(2)
    to_sib(3)
    forward(3, 2)

    rs_send(0, 0, 0)
    rs_send(1, 0, 2)
    rs_x(4).wait_recv()
    rs_send(0, 0, 1)
    rs_send(1, 0, 1)
    for o in (2, 6):
        rs_b_send(o)

    rep_x.wait()
    tot[quarter(y), :] = xhv[0] + xhv[1]

    def rep_gather(j, at):
        ref = tot.at[quarter(at)]
        return remote(ref, ref, rep_s.at[3 + j], rep_r.at[3 + j], rep(xh, (y + j) % 4))

    for j in range(1, 4):
        rep_gather(j, y).start()

    use(2, 6)

    ag_z_wait(0, 4, 0)
    ag_z_wait(0, 4, 1)
    ag_b_send(0, 4)
    ag_z_wait(1, 4, 1)
    ag_b_send(1, 4)
    sib_copy(0, 4, c).start()
    ag_z_wait(1, 4, 2)
    to_sib_other(3)
    for o in (1, 7, 0):
        rs_b_send(o)

    for p in (2, 0):
        for way in (0, 1):
            rs_send(way, 1, p)
    for o in (3, 5):
        rs_x(o).wait_recv()
    for way in (0, 1):
        rs_send(way, 1, 1)

    ag_b_wait(0, 4)
    ag_b_wait(1, 4)
    sib_copy(1, 4, c).start()
    use(3, 5)

    for p in (2, 0):
        for way in (0, 1):
            rs_send(way, 2, p)
    for o in (2, 6):
        rs_x(o).wait_recv()
    for way in (0, 1):
        rs_send(way, 2, 1)

    use(4)
    valv[...] = acc[...].astype(BF16)
    outs = [pltpu.make_async_copy(valv, val_out, out_sem.at[0])]
    outs[0].start()

    for p in (2, 0):
        for way in (0, 1):
            rs_send(way, 3, p)
    for o in (1, 7):
        rs_x(o).wait_recv()
    for way in (0, 1):
        rs_send(way, 3, 1)

    loads[5].wait()
    for j in range(1, 4):
        rep_scatter(j).wait_send()
        rep_gather(j, (y + 4 - j) % 4).wait_recv()

    @pl.loop(0, SH // BLK)
    def _(i):
        at = pl.ds(pl.multiple_of(i * BLK, BLK), BLK)
        outer = tot[at, :] * 0.125
        new = 0.9 * momv[at, :] + outer
        rpv[at, :] = new
        diff[at, :] = opv[at, :] - 0.7 * (outer + 0.9 * new)

    for way in (0, 1):
        rs_z(way, 3, 2).wait_recv()
    summed(xq.at[8], ox, z, 0, HF, [zr.at[0, 3, 2], zr.at[1, 3, 2]])
    rs_x(8).start()

    def finish(start, received):
        @pl.loop(0, HF // BLK)
        def _(i):
            at = pl.multiple_of(i * BLK, BLK)
            dwv[pl.ds(pl.multiple_of(start + at, BLK), BLK), :] = total(x, z, start, at, received) * back

    rs_x(0).wait_recv()
    for way in (0, 1):
        rs_z(way, 3, 1).wait_recv()
    finish(HF, [xr.at[0], zr.at[0, 3, 1], zr.at[1, 3, 1]])
    for way in (0, 1):
        rs_z(way, 3, 0).wait_recv()
    rs_x(8).wait_recv()
    finish(0, [xr.at[8], zr.at[0, 3, 0], zr.at[1, 3, 0]])
    outs.append(pltpu.make_async_copy(dwv, dw_out.at[0], out_sem.at[1]))
    outs[1].start()

    for k in range(1, 5):
        for way in (0, 1):
            for p in (0, 1, 2):
                if k < 4 or p == 1 or (way, p) in ((0, 0), (1, 2)):
                    ag_z(way, k, p, far(way, k - 1)).wait_send()
                j = k - 1
                if j > 0 or p == 1 or (way, p) in ((0, 0), (1, 2)):
                    rs_z(way, j, p).wait_send()
    ag_x(0, x, z, 0, HF).wait_send()
    ag_x(1, x, z, HF, HF).wait_send()
    for k in range(1, 5):
        for way in (0, 1):
            n, start, size = b_of(way, k)
            ag_x(n, x, far(way, k), start, size).wait_send()
    for n in range(9):
        rs_x(n).wait_send()
    for xrel in (0, 1):
        for o in range(NZ):
            sib_copy(xrel, o, c).wait_send()
    tok_x.wait_send()
    tok_g.wait_send()
    for j in range(1, 4):
        rep_gather(j, y).wait_send()
    outs.append(pltpu.make_async_copy(diff, np_out, out_sem.at[2]))
    outs.append(pltpu.make_async_copy(rpv, nm_out, out_sem.at[3]))
    outs[2].start()
    outs[3].start()
    pltpu.make_async_copy(dxv, dx_out, dx_sem.at[0]).wait()
    for copy in outs:
        copy.wait()


def local(grad_scale, activations, cotangent, inner_weight, outer_params, replica_params, momentum):
    tokens, width = activations.shape
    kv = cotangent.shape[1]
    any_spec = pl.BlockSpec(memory_space=pl.ANY)
    dma = pltpu.SemaphoreType.DMA
    vm = pltpu.VMEM
    return pl.pallas_call(
        functools.partial(kernel, grad_scale),
        out_shape=(
            jax.ShapeDtypeStruct((tokens, kv), BF16),
            jax.ShapeDtypeStruct((tokens, width), BF16),
            jax.ShapeDtypeStruct((1, SH, kv), F32),
            jax.ShapeDtypeStruct((SH, kv), F32),
            jax.ShapeDtypeStruct((SH, kv), F32),
        ),
        in_specs=[any_spec] * 6,
        out_specs=(any_spec,) * 5,
        scratch_shapes=[
            vm((tokens, width), BF16),
            vm((2 * tokens, width // 2), BF16),
            vm((2 * tokens, kv), BF16),
            vm((16, 2 * SH, kv), BF16),
            vm((16, SH, kv), F32),
            vm((2, 4, 3, HF, kv), BF16),
            vm((2, 4, 3, HF, kv), BF16),
            vm((9, HF, kv), BF16),
            vm((9, HF, kv), BF16),
            vm((tokens, width), BF16),
            vm((tokens, kv), F32),
            vm((tokens, kv), BF16),
            vm((SH, kv), F32),
            vm((SH, kv), F32),
            vm((SH, kv), F32),
            vm((SH, kv), F32),
            vm((SH, kv), F32),
            vm((3, QT, kv), F32),
            vm((2, QT, kv), F32),
            vm((SH, kv), F32),
            vm((8, 128), F32),
            vm((8, 128), F32),
            vm((NZ - 1, 8, 128), F32),
            dma((6,)), dma((1,)), dma((4,)), dma((1,)),
            dma((2, 4, 3)), dma((2, 4, 3)), dma((10,)), dma((10,)),
            dma((16,)), dma((16,)), dma((2,)), dma((2,)),
            dma((2, 4, 3)), dma((2, 4, 3)), dma((9,)), dma((9,)),
            dma((8,)), dma((8,)), dma((7,)), dma((7,)),
        ],
        compiler_params=pltpu.CompilerParams(
            collective_id=0, has_side_effects=True, vmem_limit_bytes=56 << 20
        ),
        name="step",
    )(activations, cotangent, inner_weight, outer_params, replica_params, momentum)


def solution(mesh):
    rows = P(("replica", "fsdp"), None)
    placed = (rows, rows, P("replica", "fsdp", None), P("fsdp", None), P("replica", "fsdp", None), P("fsdp", None))

    def run(activations, *rest):
        grad_scale = 1.0 / math.sqrt(activations.shape[0] // mesh.shape["replica"])
        return jax.shard_map(
            functools.partial(local, grad_scale),
            mesh=mesh,
            in_specs=placed,
            out_specs=(rows, rows, P("replica", "fsdp", None), P("fsdp", None), P("fsdp", None)),
            check_vma=False,
        )(activations, *rest)

    return run
```

time: 244 us -> 89.4 us (0.37)
  waiting for transfers between devices: 199 us -> 0 us
  Pallas kernels: 0 us -> 80.1 us
  matrix products: 22.7 us -> 0 us
  between operations: 15.5 us -> 0.65 us
  local copies, waits for them, and re-layouts: 0.01 us -> 8.48 us
  other arithmetic: 6.64 us -> 0 us
    reduce_scatter x1 -> x0, waiting for transfers between devices: 115 us -> none  [local(): lax.psum_scatter(lax.dot_general(feature_cols, cotangent, (((0,), (0,)),...]
    psum x1 -> x0, waiting for transfers between devices: 83.6 us -> none  [local(): outer_grad = lax.psum(difference, 'replica') / replicas]
    pallas_call x0 -> x1, Pallas kernels: none -> 80.1 us  [local(): pl.pallas_call(functools.partial(kernel, grad_scale), out_shape=(jax.Shap...]
    dot_general x3 -> x0, matrix products: 22.7 us -> none  [the longest x1 9.27 us: local(): lax.dot_general(feature_cols, cotangent, (((0,), (0,)), ((), ())), prefer...]
    unnamed x4 -> x11, local copies, waits for them, and re-layouts: 0.01 us -> 8.48 us
    sub x2 -> x0, other arithmetic: 4.75 us -> none  [the longest x1 2.54 us: local(): new_params = outer_params - 0.7 * (outer_grad + 0.9 * new_momentum)]
  transfers between devices with their start and end apart: 3 -> 0, of which waited for: 2 -> 0; matrix products, arithmetic and copies ran while one was open for 10% -> 0% of each run, Pallas kernels for 0% -> 0%
where the time goes in v1:
time: 89.4 us; the launch traced here: 89.2 us
  Pallas kernels  80.1 us (90%)
  local copies, waits for them, and re-layouts  8.48 us (9%)
    pallas_call x1, Pallas kernels, local(): pl.pallas_call(functools.partial(kernel, grad_scale), out_shape=(jax.Shap...  80.1 us
    unnamed x11, local copies, waits for them, and re-layouts  8.48 us

profile of v1, /device:TPU:16, one launch (start us, length us, event | category | flops | bytes accessed | tf_op | source)
XLA Modules:
  0.0 89.2 jit_solution(12658912760319911547)
XLA Ops:
  0.6 80.1 %step.1 = (bf16[384,1024]{1,0:T(8,128)(2,1)}, bf16[384,4096]{1,0:T(8,128)(2,1)}, f32[1,128,1024]{2,1,0:T(8,128)}, f32[128,1024]{1,0:T(8,128)}, f32[128,1024]{1,0:T(8,128)}) custom-call(bf16[384,4096]{1,0:T(8,128)(2,1)} %x_in.1, bf16[384,1024]{1,0:T(8,128)(2,1)} %g_in.1, bf16[1,128,1024]{2,1,0:T(8,128)(2,1)} %w_in.1, f32[128,1024]{1,0:T(8,128)} %op_in.1, ...), custom_call_target="tpu_custom_call" | custom-call | tf_op jit(solution)/shard_map/step/pallas_call | solution.py:499
  80.7 2.1 %copy.16 = bf16[384,1024]{1,0:T(8,128)(2,1)} copy(bf16[384,1024]{1,0:T(8,128)(2,1)} %get-tuple-element.10) | data formatting | bytes 1572864
  82.8 0.0 copy-start.2
  82.8 0.0 copy-start.1
  82.8 0.0 copy-start
  82.8 4.0 %copy.17 = bf16[384,4096]{1,0:T(8,128)(2,1)} copy(bf16[384,4096]{1,0:T(8,128)(2,1)} %get-tuple-element.11) | data formatting | bytes 6291456
  86.8 0.0 copy-done.2
  86.8 0.8 copy.18
  87.6 0.0 copy-done.1
  87.6 0.8 copy.19
  88.4 0.0 copy-done
  88.4 0.8 copy.20
Async XLA Ops:
  82.8 4.0 %copy-start.2 = (f32[1,128,1024]{2,1,0:T(8,128)S(1)}, f32[1,128,1024]{2,1,0:T(8,128)}, u32[]{:S(2)}) copy-start(f32[1,128,1024]{2,1,0:T(8,128)} %get-tuple-element.12) | copy-start | bytes 1572868
  82.8 4.8 %copy-start.1 = (f32[128,1024]{1,0:T(8,128)S(1)}, f32[128,1024]{1,0:T(8,128)}, u32[]{:S(2)}) copy-start(f32[128,1024]{1,0:T(8,128)} %get-tuple-element.13) | copy-start | bytes 1572868
  82.8 5.6 %copy-start = (f32[128,1024]{1,0:T(8,128)S(1)}, f32[128,1024]{1,0:T(8,128)}, u32[]{:S(2)}) copy-start(f32[128,1024]{1,0:T(8,128)} %get-tuple-element.14) | copy-start | bytes 1572868

commit v2 on v1

--- a/solution.py
+++ b/solution.py
@@ -36,9 +36,9 @@
     grad_scale,
     x_in, g_in, w_in, op_in, rp_in, mom_in,
     val_out, dx_out, dw_out, np_out, nm_out,
-    xv, xs, gs, W, part, zq, zr, xq, xr, dxv, acc, valv, dwv,
-    opv, rpv, momv, diff, ryv, xhv, tot, mine, mxr, mzr,
-    load_sem, xs_sem, out_sem, dx_sem,
+    xv, xs, gs, W, part, zq, zr, xq, xr, acc,
+    opv, rpv, momv, diff, ryv, xhv, tot, mine, mxr, pair, mzr,
+    load_sem, xs_sem,
     agz_s, agz_r, agx_s, agx_r, sib_s, sib_r, tok_s, tok_r,
     rsz_s, rsz_r, rsx_s, rsx_r, mx_s, mx_r, rep_s, rep_r,
 ):
@@ -177,11 +177,30 @@
     for j in range(1, 4):
         rep_scatter(j).start()
 
+    def use(xrel, *offsets):
+        for o in offsets:
+            sib_copy(xrel, o, oc).wait_recv()
+        first, step = offsets[0], offsets[-1] - offsets[0]
+
+        @pl.loop(0, len(offsets))
+        def _(t):
+            i = idx(x if xrel == 0 else ox, zmod(z + first + t * step))
+            at = pl.ds(pl.multiple_of(i * 256, 256), 256)
+            w = W[i]
+            dx_out[:, at] = lax.dot_general(
+                gs[pl.ds(0, 384), :], w, (((1,), (1,)), ((), ())), preferred_element_type=F32
+            ).astype(BF16)
+            acc[...] += jnp.dot(xv[:, at], w, preferred_element_type=F32)
+
+    acc[...] = jnp.zeros_like(acc)
+    loads[3].wait()
+    loads[4].wait()
+    use(0, 0)
+
     ag_x(0, ox, z, 0, HF).wait_recv()
     for way in (0, 1):
         ag_z_send(way, 1, 2)
 
-    loads[3].wait()
     tok_x = remote(xs.at[pl.ds(384, 384)], xs.at[pl.ds(384, 384)], tok_s.at[0], tok_r.at[0], sib)
     pltpu.make_async_copy(xs.at[pl.ds(0, 384)], xs.at[pl.ds(0, 384)], xs_sem.at[0]).wait()
     tok_g.wait_recv()
@@ -195,29 +214,6 @@
                 xs[:, at], gs[...], (((0,), (0,)), ((), ())), preferred_element_type=F32
             ).reshape(4, SH, 1024)
 
-    def use(*offsets):
-        for o in offsets:
-            for xrel in (0, 1):
-                sib_copy(xrel, o, oc).wait_recv()
-        n = len(offsets)
-        first, step = offsets[0], (offsets[1] - offsets[0] if n > 1 else 0)
-
-        @pl.loop(0, 2 * n)
-        def _(t):
-            o = first + (t // 2) * step
-            i = t % 2
-            xx = x * (1 - i) + ox * i
-            products_at(idx(xx, zmod(z + o)))
-
-    def products_at(i):
-        at = pl.ds(pl.multiple_of(i * 256, 256), 256)
-        w = W[i]
-        dxv[:, at] = lax.dot_general(
-            gs[pl.ds(0, 384), :], w, (((1,), (1,)), ((), ())), preferred_element_type=F32
-        ).astype(BF16)
-        pltpu.make_async_copy(dxv.at[:, at], dx_out.at[:, at], dx_sem.at[0]).start()
-        acc[...] += jnp.dot(xv[:, at], w, preferred_element_type=F32)
-
     def forward(k, p):
         for way in (0, 1):
             ag_z_wait(way, k, p)
@@ -238,30 +234,11 @@
             ag_b_wait(way, k)
             sib_copy(1, off(way, k), c).start()
 
-    partial(0, 2)
+    partial(0, 1)
     forward(1, 0)
-    partial(2, 3)
+    partial(1, 2)
     forward(1, 1)
     to_sib(1)
-    partial(3, 4)
-    forward(1, 2)
-
-    ag_x(1, ox, z, HF, HF).wait_recv()
-    sib_copy(1, 0, c).start()
-
-    mine[...] = jnp.zeros_like(mine)
-
-    @pl.loop(0, 16 * SH // BLK)
-    def _(i):
-        v = jnp.abs(part[i // (SH // BLK), pl.ds(pl.multiple_of((i % (SH // BLK)) * BLK, BLK), BLK), :])
-        v = jnp.maximum(v[0:8], v[8:16])
-        m = mine[...]
-        for j in range(8):
-            m = jnp.maximum(m, v[:, j * 128 : (j + 1) * 128])
-        mine[...] = m
-
-    max_x = remote(mine, mxr, mx_s.at[0], mx_r.at[0], x_nb)
-    max_x.start()
 
     for j in range(1, 4):
         rep_scatter(j).wait_recv()
@@ -269,52 +246,49 @@
     xhv[0] = tot[quarter(y), :]
     rep_x = remote(xhv.at[0], xhv.at[1], rep_s.at[3], rep_r.at[3], xh_nb)
     rep_x.start()
-
-    max_x.wait()
-    mine[...] = jnp.maximum(mine[...], mxr[...])
-
-    def max_z(j):
-        return remote(mine, mzr.at[j - 1], mx_s.at[j], mx_r.at[j], dev(x, zmod(z + j), c))
-
-    for j in range(1, NZ):
-        max_z(j).start()
-
-    acc[...] = jnp.zeros_like(acc)
-    loads[4].wait()
-    forward(2, 0)
-    to_sib_other(1)
-    use(0)
-    forward(2, 1)
-    to_sib(2)
-    use(1, 7)
-    forward(2, 2)
-
-    for j in range(1, NZ):
-        max_z(j).wait()
-    m = mine[...]
-    for j in range(NZ - 1):
-        m = jnp.maximum(m, mzr[j])
-    top = jnp.maximum(jnp.full((8, 128), jnp.max(m), F32), 1e-30)
-    scale = jnp.max(2048.0 / top)
-    back = jnp.max(top * (grad_scale / 2048.0))
-
-    def total(xx, zz, start, at, received):
-        v = part[idx(xx, zz), pl.ds(pl.multiple_of(start + at, BLK), BLK), :] * scale
-        for ref in received:
-            v = v + decode(ref[pl.ds(pl.multiple_of(at, BLK), BLK), :])
-        return v
-
-    def summed(dst, xx, zz, start, size, received):
+    partial(2, 4)
+    forward(1, 2)
+
+    ag_x(1, ox, z, HF, HF).wait_recv()
+    sib_copy(1, 0, c).start()
+
+    def largest(i, m):
+        v = jnp.abs(part[i // 2, pl.ds(pl.multiple_of((i % 2) * HF, HF), HF), :])
+        for j in range(HF // 8):
+            m = jnp.maximum(m, v[8 * j : 8 * j + 8])
+        return m
+
+    wide = lax.fori_loop(0, 32, largest, jnp.zeros((8, 1024), F32))
+    narrow = wide[:, 0:128]
+    for j in range(1, 8):
+        narrow = jnp.maximum(narrow, wide[:, j * 128 : (j + 1) * 128])
+    mine[...] = narrow
+    max_x = remote(mine, mxr, mx_s.at[0], mx_r.at[0], x_nb)
+    max_x.start()
+
+    def tile(m):
+        return jnp.maximum(jnp.full((8, 128), jnp.max(m), F32), 1e-30)
+
+    own_scale = jnp.max(2048.0 / tile(mine[...]))
+
+    def encoded(dst, xx, zz, start, size, factor, received):
         @pl.loop(0, size // BLK)
         def _(i):
             at = pl.multiple_of(i * BLK, BLK)
-            dst[pl.ds(at, BLK), :] = encode(total(xx, zz, start, at, received))
+            dst[pl.ds(at, BLK), :] = encode(total(xx, zz, start, at, factor, received))
+
+    def total(xx, zz, start, at, factor, received):
+        v = part[idx(xx, zz), pl.ds(pl.multiple_of(start + at, BLK), BLK), :] * factor
+        for ref, by in received:
+            w = decode(ref[pl.ds(pl.multiple_of(at, BLK), BLK), :])
+            v = v + (w if by is None else w * by)
+        return v
 
     def rs_x(n):
         return remote(xq.at[n], xr.at[n], rsx_s.at[n], rsx_r.at[n], x_nb)
 
     def rs_b_send(o):
-        summed(xq.at[o], ox, zmod(z + o), HF, HF, [])
+        encoded(xq.at[o], ox, zmod(z + o), HF, HF, own_scale, [])
         rs_x(o).start()
 
     def rs_z(way, j, p):
@@ -330,31 +304,62 @@
         if p != 1:
             if j > 0 and not (j == 1 and (way, p) in ((0, 2), (1, 0))):
                 rs_z(way, j - 1, p).wait_recv()
-                received = [zr.at[way, j - 1, p]]
+                received = [(zr.at[way, j - 1, p], None)]
             else:
                 received = []
-            summed(out, col, zz, 0, HF, received)
+            encoded(out, col, zz, 0, HF, scale, received)
         elif j >= 2:
             rs_z(way, j - 1, p).wait_recv()
-            summed(out, col, zz, HF, HF, [crossed, zr.at[way, j - 1, p]])
+            encoded(out, col, zz, HF, HF, scale, [(crossed, ratio), (zr.at[way, j - 1, p], None)])
         else:
             for half in (0, 1):
                 at = pl.ds(QT * half, QT)
                 if j == 0 and half == way:
-                    summed(out.at[at], col, zz, HF + QT * half, QT, [crossed.at[at]])
+                    encoded(out.at[at], col, zz, HF + QT * half, QT, scale, [(crossed.at[at], ratio)])
                 elif j == 1 and half == way:
                     rs_z(way, 0, p).wait_recv()
-                    summed(out.at[at], col, zz, HF + QT * half, QT, [crossed.at[at], zr.at[way, 0, p, at]])
+                    encoded(
+                        out.at[at], col, zz, HF + QT * half, QT, scale,
+                        [(crossed.at[at], ratio), (zr.at[way, 0, p, at], None)],
+                    )
                 elif j == 1:
-                    summed(out.at[at], col, zz, HF + QT * half, QT, [crossed.at[at]])
+                    encoded(out.at[at], col, zz, HF + QT * half, QT, scale, [(crossed.at[at], ratio)])
         rs_z(way, j, p).start()
 
     for o in (4, 3, 5):
         rs_b_send(o)
-
+    use(1, 0)
+
+    max_x.wait()
+    pair[...] = jnp.maximum(mine[...], mxr[...])
+
+    def max_z(j):
+        return remote(pair, mzr.at[j - 1], mx_s.at[j], mx_r.at[j], dev(x, zmod(z + j), c))
+
+    for j in range(1, NZ):
+        max_z(j).start()
+
+    forward(2, 0)
+    use(0, 1, 7)
+    forward(2, 1)
+    to_sib(2)
+    to_sib_other(1)
+    forward(2, 2)
+
+    for j in range(1, NZ):
+        max_z(j).wait()
+    most = pair[...]
+    for j in range(NZ - 1):
+        most = jnp.maximum(most, mzr[j])
+    top = tile(most)
+    scale = jnp.max(2048.0 / top)
+    back = jnp.max(top * (grad_scale / 2048.0))
+    ratio = jnp.max(tile(mxr[...]) / top)
+
+    use(1, 1, 7)
     forward(3, 0)
+    use(0, 2, 6)
     forward(3, 1)
-    to_sib_other(2)
     to_sib(3)
     forward(3, 2)
 
@@ -363,6 +368,8 @@
     rs_x(4).wait_recv()
     rs_send(0, 0, 1)
     rs_send(1, 0, 1)
+    rs_send(0, 1, 2)
+    rs_send(1, 1, 0)
     for o in (2, 6):
         rs_b_send(o)
 
@@ -376,56 +383,45 @@
     for j in range(1, 4):
         rep_gather(j, y).start()
 
-    use(2, 6)
-
-    ag_z_wait(0, 4, 0)
+    use(0, 3, 5)
+
     ag_z_wait(0, 4, 1)
     ag_b_send(0, 4)
     ag_z_wait(1, 4, 1)
     ag_b_send(1, 4)
+    ag_z_wait(0, 4, 0)
     sib_copy(0, 4, c).start()
     ag_z_wait(1, 4, 2)
-    to_sib_other(3)
+    to_sib_other(2)
+
+    rs_send(0, 1, 0)
+    rs_send(1, 1, 2)
+    for o in (3, 5):
+        rs_x(o).wait_recv()
+    for way in (0, 1):
+        rs_send(way, 1, 1)
     for o in (1, 7, 0):
         rs_b_send(o)
-
-    for p in (2, 0):
-        for way in (0, 1):
-            rs_send(way, 1, p)
-    for o in (3, 5):
+    use(1, 2, 6)
+    use(0, 4)
+
+    rs_send(0, 2, 2)
+    rs_send(1, 2, 0)
+    to_sib_other(3)
+    rs_send(0, 2, 0)
+    rs_send(1, 2, 2)
+    use(1, 3, 5)
+    for o in (2, 6):
         rs_x(o).wait_recv()
     for way in (0, 1):
-        rs_send(way, 1, 1)
+        rs_send(way, 2, 1)
 
     ag_b_wait(0, 4)
     ag_b_wait(1, 4)
     sib_copy(1, 4, c).start()
-    use(3, 5)
-
-    for p in (2, 0):
-        for way in (0, 1):
-            rs_send(way, 2, p)
-    for o in (2, 6):
-        rs_x(o).wait_recv()
-    for way in (0, 1):
-        rs_send(way, 2, 1)
-
-    use(4)
-    valv[...] = acc[...].astype(BF16)
-    outs = [pltpu.make_async_copy(valv, val_out, out_sem.at[0])]
-    outs[0].start()
-
-    for p in (2, 0):
-        for way in (0, 1):
-            rs_send(way, 3, p)
-    for o in (1, 7):
-        rs_x(o).wait_recv()
-    for way in (0, 1):
-        rs_send(way, 3, 1)
 
     loads[5].wait()
     for j in range(1, 4):
-        rep_scatter(j).wait_send()
         rep_gather(j, (y + 4 - j) % 4).wait_recv()
 
     @pl.loop(0, SH // BLK)
@@ -433,30 +429,41 @@
         at = pl.ds(pl.multiple_of(i * BLK, BLK), BLK)
         outer = tot[at, :] * 0.125
         new = 0.9 * momv[at, :] + outer
-        rpv[at, :] = new
-        diff[at, :] = opv[at, :] - 0.7 * (outer + 0.9 * new)
+        nm_out[at, :] = new
+        np_out[at, :] = opv[at, :] - 0.7 * (outer + 0.9 * new)
+
+    rs_send(0, 3, 2)
+    rs_send(1, 3, 2)
+    use(1, 4)
+    val_out[...] = acc[...].astype(BF16)
+    rs_send(0, 3, 0)
+    rs_send(1, 3, 0)
+    for o in (1, 7):
+        rs_x(o).wait_recv()
+    for way in (0, 1):
+        rs_send(way, 3, 1)
 
     for way in (0, 1):
         rs_z(way, 3, 2).wait_recv()
-    summed(xq.at[8], ox, z, 0, HF, [zr.at[0, 3, 2], zr.at[1, 3, 2]])
+    encoded(xq.at[8], ox, z, 0, HF, scale, [(zr.at[0, 3, 2], None), (zr.at[1, 3, 2], None)])
     rs_x(8).start()
 
     def finish(start, received):
         @pl.loop(0, HF // BLK)
         def _(i):
             at = pl.multiple_of(i * BLK, BLK)
-            dwv[pl.ds(pl.multiple_of(start + at, BLK), BLK), :] = total(x, z, start, at, received) * back
-
+            dw_out[0, pl.ds(pl.multiple_of(start + at, BLK), BLK), :] = (
+                total(x, z, start, at, scale, received) * back
+            )
+
+    rs_x(8).wait_recv()
+    for way in (0, 1):
+        rs_z(way, 3, 0).wait_recv()
+    finish(0, [(xr.at[8], None), (zr.at[0, 3, 0], None), (zr.at[1, 3, 0], None)])
     rs_x(0).wait_recv()
     for way in (0, 1):
         rs_z(way, 3, 1).wait_recv()
-    finish(HF, [xr.at[0], zr.at[0, 3, 1], zr.at[1, 3, 1]])
-    for way in (0, 1):
-        rs_z(way, 3, 0).wait_recv()
-    rs_x(8).wait_recv()
-    finish(0, [xr.at[8], zr.at[0, 3, 0], zr.at[1, 3, 0]])
-    outs.append(pltpu.make_async_copy(dwv, dw_out.at[0], out_sem.at[1]))
-    outs[1].start()
+    finish(HF, [(xr.at[0], ratio), (zr.at[0, 3, 1], None), (zr.at[1, 3, 1], None)])
 
     for k in range(1, 5):
         for way in (0, 1):
@@ -480,13 +487,15 @@
     tok_x.wait_send()
     tok_g.wait_send()
     for j in range(1, 4):
+        rep_scatter(j).wait_send()
         rep_gather(j, y).wait_send()
-    outs.append(pltpu.make_async_copy(diff, np_out, out_sem.at[2]))
-    outs.append(pltpu.make_async_copy(rpv, nm_out, out_sem.at[3]))
-    outs[2].start()
-    outs[3].start()
-    pltpu.make_async_copy(dxv, dx_out, dx_sem.at[0]).wait()
-    for copy in outs:
+
+
+def store(*refs):
+    copies = [pltpu.make_async_copy(refs[i], refs[5 + i], refs[10].at[i]) for i in range(5)]
+    for copy in copies:
+        copy.start()
+    for copy in copies:
         copy.wait()
 
 
@@ -494,19 +503,20 @@
     tokens, width = activations.shape
     kv = cotangent.shape[1]
     any_spec = pl.BlockSpec(memory_space=pl.ANY)
+    vmem_spec = pl.BlockSpec(memory_space=pltpu.VMEM)
     dma = pltpu.SemaphoreType.DMA
     vm = pltpu.VMEM
-    return pl.pallas_call(
+    results = pl.pallas_call(
         functools.partial(kernel, grad_scale),
         out_shape=(
-            jax.ShapeDtypeStruct((tokens, kv), BF16),
-            jax.ShapeDtypeStruct((tokens, width), BF16),
-            jax.ShapeDtypeStruct((1, SH, kv), F32),
-            jax.ShapeDtypeStruct((SH, kv), F32),
-            jax.ShapeDtypeStruct((SH, kv), F32),
+            vm((tokens, kv), BF16),
+            vm((tokens, width), BF16),
+            vm((1, SH, kv), F32),
+            vm((SH, kv), F32),
+            vm((SH, kv), F32),
         ),
         in_specs=[any_spec] * 6,
-        out_specs=(any_spec,) * 5,
+        out_specs=(vmem_spec,) * 5,
         scratch_shapes=[
             vm((tokens, width), BF16),
             vm((2 * tokens, width // 2), BF16),
@@ -517,10 +527,7 @@
             vm((2, 4, 3, HF, kv), BF16),
             vm((9, HF, kv), BF16),
             vm((9, HF, kv), BF16),
-            vm((tokens, width), BF16),
             vm((tokens, kv), F32),
-            vm((tokens, kv), BF16),
-            vm((SH, kv), F32),
             vm((SH, kv), F32),
             vm((SH, kv), F32),
             vm((SH, kv), F32),
@@ -528,20 +535,30 @@
             vm((3, QT, kv), F32),
             vm((2, QT, kv), F32),
             vm((SH, kv), F32),
+            vm((8, 128), F32),
             vm((8, 128), F32),
             vm((8, 128), F32),
             vm((NZ - 1, 8, 128), F32),
-            dma((6,)), dma((1,)), dma((4,)), dma((1,)),
+            dma((6,)), dma((1,)),
             dma((2, 4, 3)), dma((2, 4, 3)), dma((10,)), dma((10,)),
             dma((16,)), dma((16,)), dma((2,)), dma((2,)),
             dma((2, 4, 3)), dma((2, 4, 3)), dma((9,)), dma((9,)),
             dma((8,)), dma((8,)), dma((7,)), dma((7,)),
         ],
         compiler_params=pltpu.CompilerParams(
-            collective_id=0, has_side_effects=True, vmem_limit_bytes=56 << 20
+            collective_id=0, has_side_effects=True, vmem_limit_bytes=57 << 20
         ),
         name="step",
     )(activations, cotangent, inner_weight, outer_params, replica_params, momentum)
+    return pl.pallas_call(
+        store,
+        out_shape=[jax.ShapeDtypeStruct(v.shape, v.dtype) for v in results],
+        in_specs=[vmem_spec] * 5,
+        out_specs=[pl.BlockSpec(memory_space=pltpu.HBM)] * 5,
+        scratch_shapes=[dma((5,))],
+        compiler_params=pltpu.CompilerParams(vmem_limit_bytes=1 << 20),
+        name="store",
+    )(*[pltpu.with_memory_space_constraint(v, pltpu.VMEM) for v in results])
 
 
 def solution(mesh):

time: 89.4 us -> 76.3 us (0.85)
  local copies, waits for them, and re-layouts: 8.48 us -> 0 us
  Pallas kernels: 80.1 us -> 75.6 us
    unnamed x11 -> x0, local copies, waits for them, and re-layouts: 8.48 us -> none
    pallas_call x1 -> x2, Pallas kernels: 80.1 us -> 75.6 us  [the longest x1 73.1 us: local(): pl.pallas_call(functools.partial(kernel, grad_scale), out_shape=(vm((toke...]
where the time goes in v2:
time: 76.3 us; the launch traced here: 76.2 us
  Pallas kernels  75.6 us (99%)
    pallas_call x1, Pallas kernels, local(): pl.pallas_call(functools.partial(kernel, grad_scale), out_shape=(vm((toke...  73.1 us
    pallas_call x1, Pallas kernels, local(): pl.pallas_call(store, out_shape=[jax.ShapeDtypeStruct(v.shape, v.dtype) f...  2.46 us

profile of v2, /device:TPU:16, one launch (start us, length us, event | category | flops | bytes accessed | tf_op | source)
XLA Modules:
  0.0 76.2 jit_solution(16629295756982695264)
XLA Ops:
  0.6 73.1 %step.1 = (bf16[384,1024]{1,0:T(8,128)(2,1)S(1)}, bf16[384,4096]{1,0:T(8,128)(2,1)S(1)}, f32[1,128,1024]{2,1,0:T(8,128)S(1)}, f32[128,1024]{1,0:T(8,128)S(1)}, f32[128,1024]{1,0:T(8,128)S(1)}) custom-call(bf16[384,4096]{1,0:T(8,128)(2,1)} %x_in.1, bf16[384,1024]{1,0:T(8,128)(2,1)} %g_in.1, bf16[1,128,1024]{2,1,0:T(8,128)(2,1)} %w_in.1, f32[128,1024]{1,0:T(8,128)} %op_in.1, ...), custom_call_target="tpu_custom_call" | custom-call | tf_op jit(solution)/shard_map/step/pallas_call | solution.py:509
  73.7 2.5 %store.1 = (bf16[384,1024]{1,0:T(8,128)(2,1)}, bf16[384,4096]{1,0:T(8,128)(2,1)}, f32[1,128,1024]{2,1,0:T(8,128)}, f32[128,1024]{1,0:T(8,128)}, f32[128,1024]{1,0:T(8,128)}) custom-call(bf16[384,1024]{1,0:T(8,128)(2,1)S(1)} %get-tuple-element.10.refs_0_, bf16[384,4096]{1,0:T(8,128)(2,1)S(1)} %get-tuple-element.11.refs_1_, ...), custom_call_target="tpu_custom_call" | custom-call | tf_op jit(solution)/shard_map/store/pallas_call | solution.py:553

commit v3 on v2

v3 whole, which is shorter than its diff:
```python
import functools
import math

import jax
import jax.numpy as jnp
from jax import lax
from jax.experimental import pallas as pl
from jax.experimental.pallas import tpu as pltpu
from jax.sharding import PartitionSpec as P

MESH = pl.DeviceIdType.MESH
F32 = jnp.float32
BF16 = jnp.bfloat16

NZ = 8
SH = 128
HF = 64
QT = 32
BLK = 16


def encode(v):
    a = v * v
    b = a * a
    return (b * a * (v * jnp.abs(v))).astype(BF16)


def decode(q):
    t = q.astype(F32)
    a = lax.rsqrt(lax.rsqrt(jnp.maximum(jnp.abs(t), 1e-37)))
    r = a * lax.rsqrt(a)
    return jnp.where(t < 0, -r, r)


def kernel(
    grad_scale,
    x_in, g_in, w_in, op_in, rp_in, mom_in,
    val_out, dx_out, dw_out, np_out, nm_out,
    xv, xs, gs, W, part, zq, zr, xq, xr, acc,
    opv, rpv, momv, diff, ryv, xhv, tot, tq, tr,
    load_sem, xs_sem, tok_s, tok_r, link_s, sib_s, top_s, rep_s,
    agz_r, agx_r, sib_r, rsz_r, rsx_r, top_r, rep_r,
):
    r = lax.axis_index("replica")
    f = lax.axis_index("fsdp")
    xh, y = r // 4, r % 4
    x, z, c = f // 16, (f // 2) % NZ, f % 2
    ox, oc = 1 - x, 1 - c

    def zmod(v):
        return (v + 2 * NZ) % NZ

    def dev(xx, zz, cc):
        return (r, xx * 16 + zz * 2 + cc)

    def rep(hh, yy):
        return (hh * 4 + yy, f)

    def idx(xx, zz):
        return xx * NZ + zz

    x_nb, sib = dev(ox, z, c), dev(x, z, oc)
    z_nb = (dev(x, zmod(z + 1), c), dev(x, zmod(z - 1), c))
    xh_nb = rep(1 - xh, y)

    def remote(src, dst, ss, rs, to):
        return pltpu.make_async_remote_copy(
            src_ref=src, dst_ref=dst, send_sem=ss, recv_sem=rs, device_id=to, device_id_type=MESH
        )

    def cols(j, cc):
        return pl.ds(pl.multiple_of(j * 256 + cc * SH, SH), SH)

    loads = [
        pltpu.make_async_copy(w_in.at[0], W.at[idx(x, z), pl.ds(pl.multiple_of(c * SH, SH), SH)], load_sem.at[0]),
        pltpu.make_async_copy(op_in, opv, load_sem.at[1]),
        pltpu.make_async_copy(rp_in.at[0], rpv, load_sem.at[2]),
        pltpu.make_async_copy(g_in, gs.at[pl.ds(0, 384)], load_sem.at[3]),
        pltpu.make_async_copy(x_in, xv, load_sem.at[4]),
        pltpu.make_async_copy(mom_in, momv, load_sem.at[5]),
    ]
    for copy in loads[:4]:
        copy.start()

    barrier = pltpu.get_barrier_semaphore()
    peers = [sib, x_nb, xh_nb, *z_nb]
    peers += [rep(xh, (y + j) % 4) for j in range(1, 4)]
    for peer in peers:
        pl.semaphore_signal(barrier, inc=1, device_id=peer, device_id_type=MESH)
    pl.semaphore_wait(barrier, len(peers))

    def rows(p, k=1, way=0):
        if p == 1:
            if k == 4:
                return HF + QT * way, QT
            return HF, HF
        return 0, HF

    def wpiece(xx, zz, start, size, cc=None):
        cc = c if cc is None else cc
        return W.at[idx(xx, zz), pl.ds(pl.multiple_of(cc * SH + start, QT), size)]

    def far(way, k):
        return zmod(z - k) if way == 0 else zmod(z + k)

    def ag_z(way, k, p, at):
        start, size = rows(p, k, way)
        ref = wpiece(ox if p == 2 else x, at, start, size)
        return remote(ref, ref, link_s.at[0], agz_r.at[way, k - 1, p], z_nb[way])

    def ag_z_send(way, k, p):
        ag_z(way, k, p, far(way, k - 1)).start()

    def ag_z_wait(way, k, p):
        ag_z(way, k, p, far(way, k)).wait_recv()

    def ag_x(n, zz, start, size):
        ref = wpiece(x, zz, start, size)
        return remote(ref, ref, link_s.at[0], agx_r.at[n], x_nb)

    def ag_x_wait(n, zz, start, size):
        ref = wpiece(ox, zz, start, size)
        remote(ref, ref, link_s.at[0], agx_r.at[n], x_nb).wait_recv()

    def ag_b_send(way, k):
        start, size = rows(1, k, way)
        ag_x(1 + k, far(way, k), start, size).start()

    def ag_b_wait(k):
        ag_x_wait(1 + k, far(0, k), 0 if k < 4 else HF, SH if k < 4 else HF)

    def sib_copy(xrel, o, cc):
        ref = wpiece(x if xrel == 0 else ox, zmod(z + o), 0, SH, cc)
        n = xrel * 5 + min(o, NZ - o)
        return remote(ref, ref, sib_s.at[0], sib_r.at[n], sib)

    def sib_wait(xrel, offsets):
        if len(offsets) == 1:
            sib_copy(xrel, offsets[0], oc).wait_recv()
        else:
            ref = W.at[idx(x if xrel == 0 else ox, zmod(z + offsets[0]))]
            remote(ref, ref, sib_s.at[0], sib_r.at[xrel * 5 + offsets[0]], sib).wait_recv()

    loads[0].wait()
    ag_x(0, z, 0, HF).start()
    for way in (0, 1):
        ag_z_send(way, 1, 0)
    for way in (0, 1):
        ag_z_send(way, 1, 1)

    @pl.loop(0, 16)
    def _(j):
        at = pl.ds(pl.multiple_of(j * SH, SH), SH)
        remote(x_in.at[:, cols(j, oc)], xs.at[pl.ds(384, 384), at], tok_s.at[0], tok_r.at[0], sib).start()
        pltpu.make_async_copy(x_in.at[:, cols(j, c)], xs.at[pl.ds(0, 384), at], xs_sem.at[0]).start()

    tok_g = remote(g_in, gs.at[pl.ds(384, 384)], tok_s.at[1], tok_r.at[1], sib)
    tok_g.start()
    sib_copy(0, 0, c).start()
    loads[4].start()
    loads[5].start()

    loads[1].wait()
    loads[2].wait()

    @pl.loop(0, SH // BLK)
    def _(i):
        at = pl.ds(pl.multiple_of(i * BLK, BLK), BLK)
        diff[at, :] = opv[at, :] - rpv[at, :]

    def quarter(yy):
        return pl.ds(pl.multiple_of(yy * QT, QT), QT)

    def rep_scatter(j):
        to = (y + j) % 4
        return remote(diff.at[quarter(to)], ryv.at[j - 1], rep_s.at[0], rep_r.at[0], rep(xh, to))

    for j in range(1, 4):
        rep_scatter(j).start()

    def use(xrel, *offsets):
        sib_wait(xrel, offsets)
        first, step = offsets[0], offsets[-1] - offsets[0]

        @pl.loop(0, len(offsets))
        def _(t):
            i = idx(x if xrel == 0 else ox, zmod(z + first + t * step))
            at = pl.ds(pl.multiple_of(i * 256, 256), 256)
            w = W[i]
            dx_out[:, at] = lax.dot_general(
                gs[pl.ds(0, 384), :], w, (((1,), (1,)), ((), ())), preferred_element_type=F32
            ).astype(BF16)
            acc[...] += jnp.dot(xv[:, at], w, preferred_element_type=F32)

    acc[...] = jnp.zeros_like(acc)
    loads[3].wait()
    loads[4].wait()
    use(0, 0)

    ag_x_wait(0, z, 0, HF)
    for way in (0, 1):
        ag_z_send(way, 1, 2)
    ag_x(1, z, HF, HF).start()

    tok_x = remote(xs.at[pl.ds(384, 384)], xs.at[pl.ds(384, 384)], tok_s.at[0], tok_r.at[0], sib)
    pltpu.make_async_copy(xs.at[pl.ds(0, 384)], xs.at[pl.ds(0, 384)], xs_sem.at[0]).wait()
    tok_g.wait_recv()
    tok_x.wait_recv()

    def partial(first, last):
        @pl.loop(first, last)
        def _(i):
            at = pl.ds(pl.multiple_of(i * 512, 512), 512)
            part[pl.ds(i * 4, 4)] = lax.dot_general(
                xs[:, at], gs[...], (((0,), (0,)), ((), ())), preferred_element_type=F32
            ).reshape(4, SH, 1024)

    def forward(k, p):
        for way in (0, 1):
            ag_z_wait(way, k, p)
            if k < 3:
                ag_z_send(way, k + 1, p)
            if p == 1:
                ag_b_send(way, k)

    def off(way, k):
        return (NZ - k) % NZ if way == 0 else k

    def to_sib(k):
        for way in (0, 1):
            sib_copy(0, off(way, k), c).start()

    def to_sib_other(k):
        ag_b_wait(k)
        for way in (0, 1):
            sib_copy(1, off(way, k), c).start()

    partial(0, 1)
    forward(1, 0)
    partial(1, 2)
    forward(1, 1)
    to_sib(1)

    remote(ryv, ryv, rep_s.at[0], rep_r.at[0], xh_nb).wait_recv()
    tot[quarter(y), :] = ((diff[quarter(y), :] + ryv[0]) + ryv[1]) + ryv[2]
    xhv[0] = tot[quarter(y), :]
    rep_x = remote(xhv.at[0], xhv.at[1], rep_s.at[0], rep_r.at[1], xh_nb)
    rep_x.start()
    partial(2, 4)
    forward(1, 2)

    ag_x_wait(1, z, HF, HF)
    sib_copy(1, 0, c).start()

    def largest(i, m):
        v = jnp.abs(part[i // 2, pl.ds(pl.multiple_of((i % 2) * HF, HF), HF), :])
        for j in range(HF // 8):
            m = jnp.maximum(m, v[8 * j : 8 * j + 8])
        return m

    wide = lax.fori_loop(0, 32, largest, jnp.zeros((8, 1024), F32))
    narrow = wide[:, 0:128]
    for j in range(1, 8):
        narrow = jnp.maximum(narrow, wide[:, j * 128 : (j + 1) * 128])

    def top_copy(n, to):
        return remote(tq.at[n], tr.at[n], top_s.at[0], top_r.at[n], to)

    tq[8] = narrow
    top_copy(8, x_nb).start()

    def tile(m):
        return jnp.maximum(jnp.full((8, 128), jnp.max(m), F32), 1e-30)

    own_scale = jnp.max(2048.0 / tile(narrow))

    def encoded(dst, xx, zz, start, size, factor, received):
        @pl.loop(0, size // BLK)
        def _(i):
            at = pl.multiple_of(i * BLK, BLK)
            dst[pl.ds(at, BLK), :] = encode(total(xx, zz, start, at, factor, received))

    def total(xx, zz, start, at, factor, received):
        v = part[idx(xx, zz), pl.ds(pl.multiple_of(start + at, BLK), BLK), :] * factor
        for ref, by in received:
            w = decode(ref[pl.ds(pl.multiple_of(at, BLK), BLK), :])
            v = v + w * by
        return v

    def rs_x(n):
        return remote(xq.at[n], xr.at[n], link_s.at[0], rsx_r.at[n if n < 5 else NZ - n if n < NZ else 5], x_nb)

    def rs_x_wait(o):
        ref = xr.at[o] if o in (0, 4, 8) else xr.at[pl.ds(0, 2)]
        remote(ref, ref, link_s.at[0], rsx_r.at[o if o < 5 else 5], x_nb).wait_recv()

    def rs_b_send(o):
        encoded(xq.at[o], ox, zmod(z + o), HF, HF, own_scale, [])
        rs_x(o).start()

    def rs_z(way, j, p):
        size = QT if (j == 0 and p == 1) else HF
        at = QT * way if (j == 0 and p == 1) else 0
        here, there = zq.at[way, j, p, pl.ds(at, size)], zr.at[way, j, p, pl.ds(at, size)]
        return remote(here, there, link_s.at[0], rsz_r.at[way, j, p], z_nb[way])

    factors = {}

    def prepare(way, j):
        top, came = jnp.maximum(tq[8], tr[8]), None
        if j > 0:
            top_copy(way * 4 + j - 1, z_nb[way]).wait_recv()
            came = tr[way * 4 + j - 1]
            top = jnp.maximum(top, came)
        tq[way * 4 + j] = top
        top_copy(way * 4 + j, z_nb[way]).start()
        whole = tile(top)
        factors[way, j] = (
            jnp.max(2048.0 / whole),
            jnp.max(tile(tr[8]) / whole),
            None if came is None else jnp.max(tile(came) / whole),
        )

    def rs_send(way, j, p):
        o = 4 - j if way == 0 else (4 + j) % NZ
        zz, col = zmod(z + o), (ox if p == 2 else x)
        out, crossed = zq.at[way, j, p], xr.at[o]
        scale, by_x, by_z = factors[way, j]
        if p != 1:
            received = []
            if j > 0 and not (j == 1 and (way, p) in ((0, 2), (1, 0))):
                rs_z(way, j - 1, p).wait_recv()
                received = [(zr.at[way, j - 1, p], by_z)]
            encoded(out, col, zz, 0, HF, scale, received)
        elif j >= 2:
            rs_z(way, j - 1, p).wait_recv()
            encoded(out, col, zz, HF, HF, scale, [(crossed, by_x), (zr.at[way, j - 1, p], by_z)])
        else:
            for half in (0, 1):
                at = pl.ds(QT * half, QT)
                received = [(crossed.at[at], by_x)]
                if j == 1 and half == way:
                    rs_z(way, 0, p).wait_recv()
                    received.append((zr.at[way, 0, p, at], by_z))
                if j == 1 or half == way:
                    encoded(out.at[at], col, zz, HF + QT * half, QT, scale, received)
        rs_z(way, j, p).start()

    for o in (4, 3, 5):
        rs_b_send(o)
    use(1, 0)
    forward(2, 0)
    use(0, 1, 7)
    forward(2, 1)
    to_sib(2)
    top_copy(8, x_nb).wait_recv()
    for way in (0, 1):
        prepare(way, 0)
    rs_send(0, 0, 0)
    rs_send(1, 0, 2)
    to_sib_other(1)
    forward(2, 2)
    rs_x_wait(4)
    rs_send(0, 0, 1)
    rs_send(1, 0, 1)
    use(1, 1, 7)
    for way in (0, 1):
        prepare(way, 1)
    rs_send(0, 1, 2)
    rs_send(1, 1, 0)
    for o in (2, 6):
        rs_b_send(o)
    use(0, 2, 6)

    rep_x.wait_recv()
    tot[quarter(y), :] = xhv[0] + xhv[1]

    def rep_gather(j, at):
        ref = tot.at[quarter(at)]
        return remote(ref, ref, rep_s.at[0], rep_r.at[2], rep(xh, (y + j) % 4))

    for j in range(1, 4):
        rep_gather(j, y).start()

    rs_send(0, 1, 0)
    rs_send(1, 1, 2)
    rs_x_wait(3)
    for way in (0, 1):
        rs_send(way, 1, 1)
    forward(3, 0)
    to_sib_other(2)
    forward(3, 1)
    to_sib(3)
    use(1, 2, 6)
    forward(3, 2)
    for way in (0, 1):
        prepare(way, 2)
    rs_send(0, 2, 2)
    rs_send(1, 2, 0)
    for o in (1, 7, 0):
        rs_b_send(o)
    rs_send(0, 2, 0)
    rs_send(1, 2, 2)
    use(0, 3, 5)
    rs_x_wait(2)
    for way in (0, 1):
        rs_send(way, 2, 1)

    ag_z_send(0, 4, 1)
    ag_z_send(1, 4, 1)
    ag_z_send(0, 4, 0)
    ag_z_send(1, 4, 2)
    for way in (0, 1):
        prepare(way, 3)
    rs_send(0, 3, 2)
    rs_send(1, 3, 2)
    to_sib_other(3)
    rs_send(0, 3, 0)
    rs_send(1, 3, 0)
    use(1, 3, 5)
    rs_x_wait(1)
    for way in (0, 1):
        rs_send(way, 3, 1)
    for way in (0, 1):
        ag_z_wait(way, 4, 1)
        ag_b_send(way, 4)
    ag_z_wait(0, 4, 0)
    sib_copy(0, 4, c).start()
    ag_z_wait(1, 4, 2)
    use(0, 4)
    ag_b_wait(4)
    sib_copy(1, 4, c).start()

    loads[5].wait()
    remote(ryv, ryv, rep_s.at[0], rep_r.at[2], xh_nb).wait_recv()

    @pl.loop(0, SH // BLK)
    def _(i):
        at = pl.ds(pl.multiple_of(i * BLK, BLK), BLK)
        outer = tot[at, :] * 0.125
        new = 0.9 * momv[at, :] + outer
        nm_out[at, :] = new
        np_out[at, :] = opv[at, :] - 0.7 * (outer + 0.9 * new)

    last = jnp.maximum(tq[8], tr[8])
    for way in (0, 1):
        top_copy(way * 4 + 3, z_nb[way]).wait_recv()
        last = jnp.maximum(last, tr[way * 4 + 3])
    tq[9] = last
    top_copy(9, x_nb).start()
    whole = tile(last)
    by_way = [jnp.max(tile(tr[way * 4 + 3]) / whole) for way in (0, 1)]
    for way in (0, 1):
        rs_z(way, 3, 2).wait_recv()
    encoded(xq.at[8], ox, z, 0, HF, jnp.max(2048.0 / whole), [(zr.at[way, 3, 2], by_way[way]) for way in (0, 1)])
    rs_x(8).start()
    use(1, 4)
    val_out[...] = acc[...].astype(BF16)

    def finish(start, received, add):
        @pl.loop(0, HF // BLK)
        def _(i):
            at = pl.multiple_of(i * BLK, BLK)
            out = pl.ds(pl.multiple_of(start + at, BLK), BLK)
            v = dw_out[0, out, :] if add else part[idx(x, z), out, :] * grad_scale
            for ref, by in received:
                v = v + decode(ref[pl.ds(at, BLK), :]) * by
            dw_out[0, out, :] = v

    def back(n):
        return jnp.max(tile(tr[n]) * (grad_scale / 2048.0))

    back_z = [back(way * 4 + 3) for way in (0, 1)]
    rs_x_wait(0)
    finish(HF, [(xr.at[0], back(8))], False)
    for way in (0, 1):
        rs_z(way, 3, 0).wait_recv()
    finish(0, [(zr.at[way, 3, 0], back_z[way]) for way in (0, 1)], False)
    top_copy(9, x_nb).wait_recv()
    back_x = back(9)
    for way in (0, 1):
        rs_z(way, 3, 1).wait_recv()
    finish(HF, [(zr.at[way, 3, 1], back_z[way]) for way in (0, 1)], True)
    rs_x_wait(8)
    finish(0, [(xr.at[8], back_x)], True)

    pieces = W.at[pl.ds(0, 15)]
    remote(pieces, pieces, link_s.at[0], top_r.at[0], x_nb).wait_send()
    pieces = W.at[pl.ds(0, 8)]
    remote(pieces, pieces, sib_s.at[0], top_r.at[0], sib).wait_send()
    tok_x.wait_send()
    tok_g.wait_send()
    remote(tr, tr, top_s.at[0], top_r.at[0], x_nb).wait_send()
    pieces = part.at[pl.ds(0, 7), pl.ds(0, QT)]
    remote(pieces, pieces, rep_s.at[0], top_r.at[0], xh_nb).wait_send()


def store(*refs):
    sems = refs[10]
    copies = [pltpu.make_async_copy(refs[i], refs[5 + i], sems.at[i]) for i in (0, 2, 3, 4)]
    step = refs[1].shape[0] // 4
    for n in range(4):
        at = pl.ds(n * step, step)
        copies.insert(0, pltpu.make_async_copy(refs[1].at[at], refs[6].at[at], sems.at[5 + n]))
    for copy in copies:
        copy.start()
    for copy in copies:
        copy.wait()


def local(grad_scale, activations, cotangent, inner_weight, outer_params, replica_params, momentum):
    tokens, width = activations.shape
    kv = cotangent.shape[1]
    any_spec = pl.BlockSpec(memory_space=pl.ANY)
    vmem_spec = pl.BlockSpec(memory_space=pltpu.VMEM)
    dma = pltpu.SemaphoreType.DMA
    vm = pltpu.VMEM
    results = pl.pallas_call(
        functools.partial(kernel, grad_scale),
        out_shape=(
            vm((tokens, kv), BF16),
            vm((tokens, width), BF16),
            vm((1, SH, kv), F32),
            vm((SH, kv), F32),
            vm((SH, kv), F32),
        ),
        in_specs=[any_spec] * 6,
        out_specs=(vmem_spec,) * 5,
        scratch_shapes=[
            vm((tokens, width), BF16),
            vm((2 * tokens, width // 2), BF16),
            vm((2 * tokens, kv), BF16),
            vm((16, 2 * SH, kv), BF16),
            vm((16, SH, kv), F32),
            vm((2, 4, 3, HF, kv), BF16),
            vm((2, 4, 3, HF, kv), BF16),
            vm((9, HF, kv), BF16),
            vm((9, HF, kv), BF16),
            vm((tokens, kv), F32),
            vm((SH, kv), F32),
            vm((SH, kv), F32),
            vm((SH, kv), F32),
            vm((SH, kv), F32),
            vm((3, QT, kv), F32),
            vm((2, QT, kv), F32),
            vm((SH, kv), F32),
            vm((10, 8, 128), F32),
            vm((10, 8, 128), F32),
            dma((6,)), dma((1,)), dma((2,)), dma((2,)),
            dma((1,)), dma((1,)), dma((1,)), dma((1,)),
            dma((2, 4, 3)), dma((6,)), dma((10,)), dma((2, 4, 3)), dma((6,)), dma((10,)), dma((3,)),
        ],
        compiler_params=pltpu.CompilerParams(
            collective_id=0, has_side_effects=True, vmem_limit_bytes=57 << 20
        ),
        name="step",
    )(activations, cotangent, inner_weight, outer_params, replica_params, momentum)
    return pl.pallas_call(
        store,
        out_shape=[jax.ShapeDtypeStruct(v.shape, v.dtype) for v in results],
        in_specs=[vmem_spec] * 5,
        out_specs=[pl.BlockSpec(memory_space=pltpu.HBM)] * 5,
        scratch_shapes=[dma((9,))],
        compiler_params=pltpu.CompilerParams(vmem_limit_bytes=1 << 20),
        name="store",
    )(*[pltpu.with_memory_space_constraint(v, pltpu.VMEM) for v in results])


def solution(mesh):
    rows = P(("replica", "fsdp"), None)
    placed = (rows, rows, P("replica", "fsdp", None), P("fsdp", None), P("replica", "fsdp", None), P("fsdp", None))

    def run(activations, *rest):
        grad_scale = 1.0 / math.sqrt(activations.shape[0] // mesh.shape["replica"])
        return jax.shard_map(
            functools.partial(local, grad_scale),
            mesh=mesh,
            in_specs=placed,
            out_specs=(rows, rows, P("replica", "fsdp", None), P("fsdp", None), P("fsdp", None)),
            check_vma=False,
        )(activations, *rest)

    return run
```

time: 76.3 us -> 74.7 us (0.979); the launches traced: 76.2 us -> 73.3 us
  Pallas kernels: 75.6 us -> 72.7 us
    pallas_call x1, Pallas kernels: 73.1 us -> 70.2 us  [local(): pl.pallas_call(functools.partial(kernel, grad_scale), out_shape=(vm((toke...]
where the time goes in v3:
time: 74.7 us; the launch traced here: 73.3 us
  Pallas kernels  72.7 us (97%)
    pallas_call x1, Pallas kernels, local(): pl.pallas_call(functools.partial(kernel, grad_scale), out_shape=(vm((toke...  70.2 us
    pallas_call x1, Pallas kernels, local(): pl.pallas_call(store, out_shape=[jax.ShapeDtypeStruct(v.shape, v.dtype) f...  2.5 us

profile of v3, /device:TPU:16, one launch (start us, length us, event | category | flops | bytes accessed | tf_op | source)
XLA Modules:
  0.0 73.3 jit_solution(4987506296070955936)
XLA Ops:
  0.6 70.2 %step.1 = (bf16[384,1024]{1,0:T(8,128)(2,1)S(1)}, bf16[384,4096]{1,0:T(8,128)(2,1)S(1)}, f32[1,128,1024]{2,1,0:T(8,128)S(1)}, f32[128,1024]{1,0:T(8,128)S(1)}, f32[128,1024]{1,0:T(8,128)S(1)}) custom-call(bf16[384,4096]{1,0:T(8,128)(2,1)} %x_in.1, bf16[384,1024]{1,0:T(8,128)(2,1)} %g_in.1, bf16[1,128,1024]{2,1,0:T(8,128)(2,1)} %w_in.1, f32[128,1024]{1,0:T(8,128)} %op_in.1, ...), custom_call_target="tpu_custom_call" | custom-call | tf_op jit(solution)/shard_map/step/pallas_call | solution.py:518
  70.8 2.5 %store.1 = (bf16[384,1024]{1,0:T(8,128)(2,1)}, bf16[384,4096]{1,0:T(8,128)(2,1)}, f32[1,128,1024]{2,1,0:T(8,128)}, f32[128,1024]{1,0:T(8,128)}, f32[128,1024]{1,0:T(8,128)}) custom-call(bf16[384,1024]{1,0:T(8,128)(2,1)S(1)} %get-tuple-element.10.refs_0_, bf16[384,4096]{1,0:T(8,128)(2,1)S(1)} %get-tuple-element.11.refs_1_, ...), custom_call_target="tpu_custom_call" | custom-call | tf_op jit(solution)/shard_map/store/pallas_call | solution.py:558

commit v4 on v3

--- a/solution.py
+++ b/solution.py
@@ -13,9 +13,11 @@
 BF16 = jnp.bfloat16
 
 NZ = 8
+LOW = 48
 SH = 128
 HF = 64
 QT = 32
+FIRST = ((0, 0), (1, 2), (1, 1))
 BLK = 16
 
 
@@ -61,7 +63,7 @@
 
     x_nb, sib = dev(ox, z, c), dev(x, z, oc)
     z_nb = (dev(x, zmod(z + 1), c), dev(x, zmod(z - 1), c))
-    xh_nb = rep(1 - xh, y)
+    outer = ((1 - xh) * 4 + y, ox * 16 + z * 2 + c)
 
     def remote(src, dst, ss, rs, to):
         return pltpu.make_async_remote_copy(
@@ -83,28 +85,26 @@
         copy.start()
 
     barrier = pltpu.get_barrier_semaphore()
-    peers = [sib, x_nb, xh_nb, *z_nb]
+    peers = [sib, x_nb, outer, *z_nb]
     peers += [rep(xh, (y + j) % 4) for j in range(1, 4)]
     for peer in peers:
         pl.semaphore_signal(barrier, inc=1, device_id=peer, device_id_type=MESH)
     pl.semaphore_wait(barrier, len(peers))
 
-    def rows(p, k=1, way=0):
+    def rows(p, way):
         if p == 1:
-            if k == 4:
-                return HF + QT * way, QT
             return HF, HF
-        return 0, HF
+        return 0, (LOW if p == 2 and way == 1 else HF)
 
     def wpiece(xx, zz, start, size, cc=None):
         cc = c if cc is None else cc
-        return W.at[idx(xx, zz), pl.ds(pl.multiple_of(cc * SH + start, QT), size)]
+        return W.at[idx(xx, zz), pl.ds(pl.multiple_of(cc * SH + start, BLK), size)]
 
     def far(way, k):
         return zmod(z - k) if way == 0 else zmod(z + k)
 
     def ag_z(way, k, p, at):
-        start, size = rows(p, k, way)
+        start, size = rows(p, way)
         ref = wpiece(ox if p == 2 else x, at, start, size)
         return remote(ref, ref, link_s.at[0], agz_r.at[way, k - 1, p], z_nb[way])
 
@@ -123,11 +123,12 @@
         remote(ref, ref, link_s.at[0], agx_r.at[n], x_nb).wait_recv()
 
     def ag_b_send(way, k):
-        start, size = rows(1, k, way)
-        ag_x(1 + k, far(way, k), start, size).start()
+        start = LOW if way == 1 else HF
+        ag_x(1 + k, far(way, k), start, SH - start).start()
 
     def ag_b_wait(k):
-        ag_x_wait(1 + k, far(0, k), 0 if k < 4 else HF, SH if k < 4 else HF)
+        ref = W.at[idx(ox, far(0, k)), pl.ds(0, 2 * SH - LOW - HF if k < 4 else SH - LOW)]
+        remote(ref, ref, link_s.at[0], agx_r.at[1 + k], x_nb).wait_recv()
 
     def sib_copy(xrel, o, cc):
         ref = wpiece(x if xrel == 0 else ox, zmod(z + o), 0, SH, cc)
@@ -145,6 +146,7 @@
     ag_x(0, z, 0, HF).start()
     for way in (0, 1):
         ag_z_send(way, 1, 0)
+    ag_x(1, z, HF, HF).start()
     for way in (0, 1):
         ag_z_send(way, 1, 1)
 
@@ -200,7 +202,6 @@
     ag_x_wait(0, z, 0, HF)
     for way in (0, 1):
         ag_z_send(way, 1, 2)
-    ag_x(1, z, HF, HF).start()
 
     tok_x = remote(xs.at[pl.ds(384, 384)], xs.at[pl.ds(384, 384)], tok_s.at[0], tok_r.at[0], sib)
     pltpu.make_async_copy(xs.at[pl.ds(0, 384)], xs.at[pl.ds(0, 384)], xs_sem.at[0]).wait()
@@ -218,7 +219,7 @@
     def forward(k, p):
         for way in (0, 1):
             ag_z_wait(way, k, p)
-            if k < 3:
+            if k < 3 or (way, p) in ((0, 0), (1, 1), (1, 2)):
                 ag_z_send(way, k + 1, p)
             if p == 1:
                 ag_b_send(way, k)
@@ -241,11 +242,11 @@
     forward(1, 1)
     to_sib(1)
 
-    remote(ryv, ryv, rep_s.at[0], rep_r.at[0], xh_nb).wait_recv()
+    remote(ryv, ryv, rep_s.at[0], rep_r.at[0], outer).wait_recv()
     tot[quarter(y), :] = ((diff[quarter(y), :] + ryv[0]) + ryv[1]) + ryv[2]
     xhv[0] = tot[quarter(y), :]
-    rep_x = remote(xhv.at[0], xhv.at[1], rep_s.at[0], rep_r.at[1], xh_nb)
-    rep_x.start()
+    rep_out = remote(xhv.at[0], xhv.at[1], rep_s.at[0], rep_r.at[1], outer)
+    rep_out.start()
     partial(2, 4)
     forward(1, 2)
 
@@ -299,9 +300,7 @@
         rs_x(o).start()
 
     def rs_z(way, j, p):
-        size = QT if (j == 0 and p == 1) else HF
-        at = QT * way if (j == 0 and p == 1) else 0
-        here, there = zq.at[way, j, p, pl.ds(at, size)], zr.at[way, j, p, pl.ds(at, size)]
+        here, there = zq.at[way, j, p], zr.at[way, j, p]
         return remote(here, there, link_s.at[0], rsz_r.at[way, j, p], z_nb[way])
 
     factors = {}
@@ -326,24 +325,11 @@
         zz, col = zmod(z + o), (ox if p == 2 else x)
         out, crossed = zq.at[way, j, p], xr.at[o]
         scale, by_x, by_z = factors[way, j]
-        if p != 1:
-            received = []
-            if j > 0 and not (j == 1 and (way, p) in ((0, 2), (1, 0))):
-                rs_z(way, j - 1, p).wait_recv()
-                received = [(zr.at[way, j - 1, p], by_z)]
-            encoded(out, col, zz, 0, HF, scale, received)
-        elif j >= 2:
+        start, received = (HF, [(crossed, by_x)]) if p == 1 else (0, [])
+        if j > 1 or (j == 1 and (way, p) in FIRST):
             rs_z(way, j - 1, p).wait_recv()
-            encoded(out, col, zz, HF, HF, scale, [(crossed, by_x), (zr.at[way, j - 1, p], by_z)])
-        else:
-            for half in (0, 1):
-                at = pl.ds(QT * half, QT)
-                received = [(crossed.at[at], by_x)]
-                if j == 1 and half == way:
-                    rs_z(way, 0, p).wait_recv()
-                    received.append((zr.at[way, 0, p, at], by_z))
-                if j == 1 or half == way:
-                    encoded(out.at[at], col, zz, HF + QT * half, QT, scale, received)
+            received.append((zr.at[way, j - 1, p], by_z))
+        encoded(out, col, zz, start, HF, scale, received)
         rs_z(way, j, p).start()
 
     for o in (4, 3, 5):
@@ -361,26 +347,18 @@
     to_sib_other(1)
     forward(2, 2)
     rs_x_wait(4)
-    rs_send(0, 0, 1)
     rs_send(1, 0, 1)
     use(1, 1, 7)
     for way in (0, 1):
         prepare(way, 1)
     rs_send(0, 1, 2)
     rs_send(1, 1, 0)
+    rep_out.wait_recv()
+    rep_in = remote(xhv.at[1], xhv.at[2], rep_s.at[0], rep_r.at[3], x_nb)
+    rep_in.start()
     for o in (2, 6):
         rs_b_send(o)
     use(0, 2, 6)
-
-    rep_x.wait_recv()
-    tot[quarter(y), :] = xhv[0] + xhv[1]
-
-    def rep_gather(j, at):
-        ref = tot.at[quarter(at)]
-        return remote(ref, ref, rep_s.at[0], rep_r.at[2], rep(xh, (y + j) % 4))
-
-    for j in range(1, 4):
-        rep_gather(j, y).start()
 
     rs_send(0, 1, 0)
     rs_send(1, 1, 2)
@@ -397,7 +375,7 @@
         prepare(way, 2)
     rs_send(0, 2, 2)
     rs_send(1, 2, 0)
-    for o in (1, 7, 0):
+    for o in (1, 7):
         rs_b_send(o)
     rs_send(0, 2, 0)
     rs_send(1, 2, 2)
@@ -406,10 +384,23 @@
     for way in (0, 1):
         rs_send(way, 2, 1)
 
-    ag_z_send(0, 4, 1)
-    ag_z_send(1, 4, 1)
-    ag_z_send(0, 4, 0)
-    ag_z_send(1, 4, 2)
+    rep_in.wait_recv()
+    tot[quarter(y), :] = xhv[0] + xhv[2]
+
+    def rep_gather(j, at):
+        ref = tot.at[quarter(at)]
+        return remote(ref, ref, rep_s.at[0], rep_r.at[2], rep(xh, (y + j) % 4))
+
+    for j in range(1, 4):
+        rep_gather(j, y).start()
+
+    ag_z_wait(0, 4, 0)
+    ag_z_wait(1, 4, 1)
+    ag_b_send(1, 4)
+    sib_copy(0, 4, c).start()
+    ag_z_wait(1, 4, 2)
+    rs_b_send(0)
+
     for way in (0, 1):
         prepare(way, 3)
     rs_send(0, 3, 2)
@@ -421,18 +412,12 @@
     rs_x_wait(1)
     for way in (0, 1):
         rs_send(way, 3, 1)
-    for way in (0, 1):
-        ag_z_wait(way, 4, 1)
-        ag_b_send(way, 4)
-    ag_z_wait(0, 4, 0)
-    sib_copy(0, 4, c).start()
-    ag_z_wait(1, 4, 2)
     use(0, 4)
     ag_b_wait(4)
     sib_copy(1, 4, c).start()
 
     loads[5].wait()
-    remote(ryv, ryv, rep_s.at[0], rep_r.at[2], xh_nb).wait_recv()
+    remote(ryv, ryv, rep_s.at[0], rep_r.at[2], outer).wait_recv()
 
     @pl.loop(0, SH // BLK)
     def _(i):
@@ -454,8 +439,6 @@
         rs_z(way, 3, 2).wait_recv()
     encoded(xq.at[8], ox, z, 0, HF, jnp.max(2048.0 / whole), [(zr.at[way, 3, 2], by_way[way]) for way in (0, 1)])
     rs_x(8).start()
-    use(1, 4)
-    val_out[...] = acc[...].astype(BF16)
 
     def finish(start, received, add):
         @pl.loop(0, HF // BLK)
@@ -476,6 +459,8 @@
     for way in (0, 1):
         rs_z(way, 3, 0).wait_recv()
     finish(0, [(zr.at[way, 3, 0], back_z[way]) for way in (0, 1)], False)
+    use(1, 4)
+    val_out[...] = acc[...].astype(BF16)
     top_copy(9, x_nb).wait_recv()
     back_x = back(9)
     for way in (0, 1):
@@ -491,8 +476,8 @@
     tok_x.wait_send()
     tok_g.wait_send()
     remote(tr, tr, top_s.at[0], top_r.at[0], x_nb).wait_send()
-    pieces = part.at[pl.ds(0, 7), pl.ds(0, QT)]
-    remote(pieces, pieces, rep_s.at[0], top_r.at[0], xh_nb).wait_send()
+    pieces = part.at[pl.ds(0, 8), pl.ds(0, QT)]
+    remote(pieces, pieces, rep_s.at[0], top_r.at[0], outer).wait_send()
 
 
 def store(*refs):
@@ -542,13 +527,13 @@
             vm((SH, kv), F32),
             vm((SH, kv), F32),
             vm((3, QT, kv), F32),
-            vm((2, QT, kv), F32),
+            vm((3, QT, kv), F32),
             vm((SH, kv), F32),
             vm((10, 8, 128), F32),
             vm((10, 8, 128), F32),
             dma((6,)), dma((1,)), dma((2,)), dma((2,)),
             dma((1,)), dma((1,)), dma((1,)), dma((1,)),
-            dma((2, 4, 3)), dma((6,)), dma((10,)), dma((2, 4, 3)), dma((6,)), dma((10,)), dma((3,)),
+            dma((2, 4, 3)), dma((6,)), dma((10,)), dma((2, 4, 3)), dma((6,)), dma((10,)), dma((4,)),
         ],
         compiler_params=pltpu.CompilerParams(
             collective_id=0, has_side_effects=True, vmem_limit_bytes=57 << 20

time: 74.7 us -> 72.2 us (0.967)
  Pallas kernels: 72.7 us -> 70.4 us
    pallas_call x1, Pallas kernels: 70.2 us -> 67.9 us  [local(): pl.pallas_call(functools.partial(kernel, grad_scale), out_shape=(vm((toke...]
where the time goes in v4:
time: 72.2 us; the launch traced here: 71 us
  Pallas kernels  70.4 us (98%)
    pallas_call x1, Pallas kernels, local(): pl.pallas_call(functools.partial(kernel, grad_scale), out_shape=(vm((toke...  67.9 us
    pallas_call x1, Pallas kernels, local(): pl.pallas_call(store, out_shape=[jax.ShapeDtypeStruct(v.shape, v.dtype) f...  2.5 us

profile of v4, /device:TPU:16, one launch (start us, length us, event | category | flops | bytes accessed | tf_op | source)
XLA Modules:
  0.0 71.0 jit_solution(12117331008544359049)
XLA Ops:
  0.6 67.9 %step.1 = (bf16[384,1024]{1,0:T(8,128)(2,1)S(1)}, bf16[384,4096]{1,0:T(8,128)(2,1)S(1)}, f32[1,128,1024]{2,1,0:T(8,128)S(1)}, f32[128,1024]{1,0:T(8,128)S(1)}, f32[128,1024]{1,0:T(8,128)S(1)}) custom-call(bf16[384,4096]{1,0:T(8,128)(2,1)} %x_in.1, bf16[384,1024]{1,0:T(8,128)(2,1)} %g_in.1, bf16[1,128,1024]{2,1,0:T(8,128)(2,1)} %w_in.1, f32[128,1024]{1,0:T(8,128)} %op_in.1, ...), custom_call_target="tpu_custom_call" | custom-call | tf_op jit(solution)/shard_map/step/pallas_call | solution.py:503
  68.5 2.5 %store.1 = (bf16[384,1024]{1,0:T(8,128)(2,1)}, bf16[384,4096]{1,0:T(8,128)(2,1)}, f32[1,128,1024]{2,1,0:T(8,128)}, f32[128,1024]{1,0:T(8,128)}, f32[128,1024]{1,0:T(8,128)}) custom-call(bf16[384,1024]{1,0:T(8,128)(2,1)S(1)} %get-tuple-element.10.refs_0_, bf16[384,4096]{1,0:T(8,128)(2,1)S(1)} %get-tuple-element.11.refs_1_, ...), custom_call_target="tpu_custom_call" | custom-call | tf_op jit(solution)/shard_map/store/pallas_call | solution.py:543
